TPU v7x, 32 devices: a whole 2x2x4 slice. The times are simulated.
32 devices in a mesh: dp: 8 (over z, x), tensor: 4 (over y, core).
Axes of the slice: x: 2, y: 2, z: 4, core: 2. Of those that a mesh axis runs over, the one named last changes fastest.
Arguments:
- tokens: bfloat16 [8192, 768], P(('dp', 'tensor')), may hold values from -6 to 6
- cotangent: bfloat16 [8192, 768], P(('dp', 'tensor')), may hold values from -6 to 6
- lengths: int32 [8, 4], P('dp'), may hold values from 0 to 1024, as said below
- timesteps: int32 [8, 4], P('dp'), may hold values from 0 to 999
- w_self: bfloat16 [1536, 768], replicated, may hold values from -0.15625 to 0.15625
- ln_gain: float32 [2, 768], replicated, may hold values from 0.5 to 1.5
- ln_bias: float32 [2, 768], replicated, may hold values from -1.8 to 1.8
- w_qkv: bfloat16 [2, 3, 768, 768], P(None, None, None, 'tensor'), may hold values from -0.21875 to 0.21875
- w_out: bfloat16 [2, 768, 768], P(None, 'tensor'), may hold values from -0.875 to 0.875
- w_ada: float32 [2, 768, 1536], replicated, may hold values from -0.21875 to 0.21875
- b_ada: float32 [2, 1536], replicated, may hold values from -1.8 to 1.8
- w_up: bfloat16 [2, 768, 3072], P(None, None, 'tensor'), may hold values from -0.21875 to 0.21875
- w_down: bfloat16 [2, 3072, 768], P(None, 'tensor'), may hold values from -0.109375 to 0.109375
- b_down: float32 [2, 768], replicated, may hold values from -1.8 to 1.8
Outputs:
- activations: bfloat16 [8192, 768], P(('dp', 'tensor'))
- grad_tokens: float32 [8192, 768], P(('dp', 'tensor'))
- grad_ln_gain: float32 [2, 768], replicated
- grad_ln_bias: float32 [2, 768], replicated
- grad_qkv: float32 [2, 3, 768, 768], P(None, None, 'dp', 'tensor')
- grad_out: float32 [2, 768, 768], P(None, 'tensor', 'dp')
- grad_ada: float32 [2, 768, 1536], replicated
- grad_ada_bias: float32 [2, 1536], replicated
- grad_up: float32 [2, 768, 3072], P(None, 'dp', 'tensor')
- grad_down: float32 [2, 3072, 768], P(None, 'tensor', 'dp')
- grad_down_bias: float32 [2, 768], replicated
- grad_self: float32 [1536, 768], replicated
Inputs may be any that keep to these rules, and one draw needn't show every extreme that they name: `lengths`: each row is either one sequence of 1024 tokens followed by zeros, or 4 sequences of 256 tokens; at least one row is of the first kind.
All inputs are finite; a program needn't handle non-finite values.
Results may differ from a plain program's by a relative error of at most 0.018.
Values may be sent and summed in bfloat16 or wider, within the bound.
A program may use at most 192 MiB of HBM per device.

v0:
```python
import jax
import jax.numpy as jnp
from jax import lax
from jax.sharding import PartitionSpec as P

HD = 64


def layout(lengths, index):
    ends = jnp.cumsum(lengths, axis=-1)
    starts = ends - lengths
    segment = jnp.sum((index[:, None] >= ends[..., None, :]).astype(jnp.int32), axis=-1)
    segment = jnp.minimum(segment, lengths.shape[-1] - 1)
    onehot = (segment[..., None] == jnp.arange(lengths.shape[-1], dtype=jnp.int32)).astype(
        jnp.int32
    )
    position = index - jnp.sum(onehot * starts[..., None, :], axis=-1)
    return (segment, onehot, position)


def embed_time(steps, width):
    half = width // 2
    freqs = jnp.exp(-jnp.log(10000.0) * jnp.arange(half).astype(jnp.float32) / half)
    angle = steps.astype(jnp.float32)[..., None] * freqs
    return jnp.concatenate([jnp.cos(angle), jnp.sin(angle)], axis=-1)


def rotary_tables(position, head_size):
    half = head_size // 2
    freqs = jnp.exp(-jnp.log(10000.0) * jnp.arange(half).astype(jnp.float32) / half)
    angle = position.astype(jnp.float32)[..., None] * freqs
    return (jnp.cos(angle), jnp.sin(angle))


def rotate(values, cosine, sine):
    half = values.shape[-1] // 2
    first = values[..., :half]
    second = values[..., half:]
    cosine = cosine[..., None, :]
    sine = sine[..., None, :]
    return jnp.concatenate(
        [first * cosine - second * sine, second * cosine + first * sine], axis=-1
    )


def normalize(rows):
    centred = rows - jnp.mean(rows, axis=-1, keepdims=True)
    variance = jnp.mean(centred * centred, axis=-1, keepdims=True)
    return centred * lax.rsqrt(variance + 1e-05)


def layer_norm(rows, gain, bias):
    return normalize(rows) * gain + bias


def modulate(rows, cond_rows):
    width = rows.shape[-1]
    return normalize(rows) * (1.0 + cond_rows[:, width:]) + cond_rows[:, :width]


def gelu_exact(values):
    return jax.nn.gelu(values, approximate=False)


def attend_forward(queries, key_rows, value_rows, same):
    length = queries.shape[0]
    block = min(512, length)
    count = length // block
    scale = HD ** (-0.5)
    query_blocks = queries.reshape(count, block, queries.shape[1], HD)
    mask_blocks = same.reshape(count, block, length)

    def one_block(args):
        query_part, mask_part = args
        scores = (
            jnp.einsum("qhd,khd->hqk", query_part, key_rows, preferred_element_type=jnp.float32)
            * scale
        )
        scores = jnp.where(mask_part[None], scores, -1000000000.0)
        largest = jnp.max(scores, axis=-1, keepdims=True)
        shares = jnp.exp(scores - largest)
        totals = jnp.sum(shares, axis=-1, keepdims=True)
        shares = shares / totals
        output = jnp.einsum(
            "hqk,khd->qhd",
            shares.astype(jnp.bfloat16),
            value_rows,
            preferred_element_type=jnp.float32,
        )
        return (output, (largest + jnp.log(totals))[..., 0])

    output, logsum = lax.map(one_block, (query_blocks, mask_blocks))
    return (output.reshape(length, queries.shape[1], HD), logsum)


def attend_backward(queries, key_rows, value_rows, grad_out, logsum, same):
    length = queries.shape[0]
    block = min(512, length)
    count = length // block
    scale = HD ** (-0.5)
    heads = queries.shape[1]
    query_blocks = queries.reshape(count, block, heads, HD)
    grad_blocks = grad_out.reshape(count, block, heads, HD)
    mask_blocks = same.reshape(count, block, length)

    def one_block(carry, args):
        key_grad, value_grad = carry
        query_part, grad_part, mask_part, logsum_part = args
        scores = (
            jnp.einsum("qhd,khd->hqk", query_part, key_rows, preferred_element_type=jnp.float32)
            * scale
        )
        scores = jnp.where(mask_part[None], scores, -1000000000.0)
        shares = jnp.exp(scores - logsum_part[..., None])
        grad_shares = jnp.einsum(
            "qhd,khd->hqk", grad_part, value_rows, preferred_element_type=jnp.float32
        )
        centre = jnp.sum(shares * grad_shares, axis=-1, keepdims=True)
        grad_scores = (shares * (grad_shares - centre)).astype(jnp.bfloat16)
        query_grad = (
            jnp.einsum("hqk,khd->qhd", grad_scores, key_rows, preferred_element_type=jnp.float32)
            * scale
        )
        key_grad = (
            key_grad
            + jnp.einsum(
                "hqk,qhd->khd", grad_scores, query_part, preferred_element_type=jnp.float32
            )
            * scale
        )
        value_grad = value_grad + jnp.einsum(
            "hqk,qhd->khd",
            shares.astype(jnp.bfloat16),
            grad_part,
            preferred_element_type=jnp.float32,
        )
        return ((key_grad, value_grad), query_grad)

    empty = jnp.zeros((length, heads, HD), jnp.float32)
    (key_grad, value_grad), query_grad = lax.scan(
        one_block, (empty, empty), (query_blocks, grad_blocks, mask_blocks, logsum)
    )
    return (query_grad.reshape(length, heads, HD), key_grad, value_grad)


def local(
    tokens,
    cotangent,
    lengths,
    timesteps,
    w_self,
    ln_gain,
    ln_bias,
    w_qkv,
    w_out,
    w_ada,
    b_ada,
    w_up,
    w_down,
    b_down,
):
    hp = lax.Precision.HIGHEST
    tok_rows = tokens.shape[0]
    width = tokens.shape[1]
    depth = w_qkv.shape[0]
    members = lax.axis_size("tensor")
    length = tok_rows * members
    offset = lax.axis_index("tensor") * tok_rows
    index = jnp.arange(length, dtype=jnp.int32)
    segment, onehot, position = layout(lengths[0], index)
    same = segment[:, None] == segment[None, :]
    onehot_local = lax.dynamic_slice_in_dim(onehot, offset, tok_rows, 0).astype(jnp.float32)
    cosine, sine = rotary_tables(position, HD)
    temb = embed_time(timesteps[0], width)
    heads = w_qkv.shape[3] // HD

    def run_layers(rows):
        saved = []
        for layer in range(depth):
            normed = layer_norm(rows, ln_gain[layer], ln_bias[layer]).astype(jnp.bfloat16)
            normed_all = lax.all_gather(normed, "tensor", axis=0, tiled=True)
            mixed = jnp.einsum(
                "gd,jde->jge", normed_all, w_qkv[layer], preferred_element_type=jnp.float32
            )
            queries = rotate(mixed[0].reshape(length, heads, HD), cosine, sine).astype(jnp.bfloat16)
            key_rows = rotate(mixed[1].reshape(length, heads, HD), cosine, sine).astype(
                jnp.bfloat16
            )
            value_rows = mixed[2].reshape(length, heads, HD).astype(jnp.bfloat16)
            attended, logsum = attend_forward(queries, key_rows, value_rows, same)
            attended = attended.reshape(length, heads * HD).astype(jnp.bfloat16)
            out_weight = w_out[layer]
            after = rows + lax.psum_scatter(
                jnp.dot(attended, out_weight, preferred_element_type=jnp.float32).astype(
                    jnp.bfloat16
                ),
                "tensor",
                scatter_dimension=0,
                tiled=True,
            ).astype(jnp.float32)
            cond = jnp.dot(temb, w_ada[layer], precision=hp) + b_ada[layer]
            cond_rows = jnp.dot(onehot_local, cond, precision=hp)
            modulated = modulate(after, cond_rows).astype(jnp.bfloat16)
            modulated_all = lax.all_gather(modulated, "tensor", axis=0, tiled=True)
            hidden = jnp.dot(modulated_all, w_up[layer], preferred_element_type=jnp.float32)
            gated = gelu_exact(hidden).astype(jnp.bfloat16)
            down_weight = w_down[layer]
            saved.append(
                (
                    rows,
                    normed_all,
                    queries,
                    key_rows,
                    value_rows,
                    logsum,
                    attended,
                    after,
                    cond_rows,
                    modulated_all,
                    hidden,
                    gated,
                )
            )
            rows = (
                after
                + lax.psum_scatter(
                    jnp.dot(gated, down_weight, preferred_element_type=jnp.float32).astype(
                        jnp.bfloat16
                    ),
                    "tensor",
                    scatter_dimension=0,
                    tiled=True,
                ).astype(jnp.float32)
                + b_down[layer]
            )
        return (rows, saved)

    self_top = w_self[:width]
    first_rows, unused = run_layers(jnp.dot(tokens, self_top, preferred_element_type=jnp.float32))
    joined = jnp.concatenate([tokens, first_rows.astype(jnp.bfloat16)], axis=1)
    rows, saved = run_layers(jnp.dot(joined, w_self, preferred_element_type=jnp.float32))
    activations = rows.astype(jnp.bfloat16)
    grad_rows = cotangent.astype(jnp.float32)
    qkv_list = [None] * depth
    out_list = [None] * depth
    up_list = [None] * depth
    down_list = [None] * depth
    slot_list = [None] * depth
    gain_list = [None] * depth
    bias_list = [None] * depth
    down_bias_list = [None] * depth
    for layer in reversed(range(depth)):
        (
            rows_in,
            normed_all,
            queries,
            key_rows,
            value_rows,
            logsum,
            attended,
            after,
            cond_rows,
            modulated_all,
            hidden,
            gated,
        ) = saved[layer]
        down_bias_list[layer] = jnp.sum(grad_rows, axis=0)
        grad_all = lax.all_gather(grad_rows.astype(jnp.bfloat16), "tensor", axis=0, tiled=True)
        grad_down = jnp.dot(gated.T, grad_all, preferred_element_type=jnp.float32)
        grad_gated = jnp.dot(grad_all, w_down[layer].T, preferred_element_type=jnp.float32)
        gelu_pull = jax.vjp(gelu_exact, hidden)[1]
        grad_hidden = gelu_pull(grad_gated)[0].astype(jnp.bfloat16)
        grad_up = jnp.dot(modulated_all.T, grad_hidden, preferred_element_type=jnp.float32)
        up_weight = w_up[layer]
        grad_modulated = lax.psum_scatter(
            jnp.dot(grad_hidden, up_weight.T, preferred_element_type=jnp.float32).astype(
                jnp.bfloat16
            ),
            "tensor",
            scatter_dimension=0,
            tiled=True,
        ).astype(jnp.float32)
        modulate_pull = jax.vjp(modulate, after, cond_rows)[1]
        grad_after_mod, grad_cond = modulate_pull(grad_modulated)
        grad_after = grad_rows + grad_after_mod
        slot_list[layer] = jnp.dot(onehot_local.T, grad_cond, precision=hp)
        grad_after_all = lax.all_gather(
            grad_after.astype(jnp.bfloat16), "tensor", axis=0, tiled=True
        )
        grad_out = jnp.dot(attended.T, grad_after_all, preferred_element_type=jnp.float32)
        grad_attended = jnp.dot(grad_after_all, w_out[layer].T, preferred_element_type=jnp.float32)
        grad_attended = grad_attended.astype(jnp.bfloat16).reshape(length, heads, HD)
        grad_queries, grad_keys, grad_values = attend_backward(
            queries, key_rows, value_rows, grad_attended, logsum, same
        )
        grad_queries = rotate(grad_queries, cosine, -sine)
        grad_keys = rotate(grad_keys, cosine, -sine)
        grad_mixed = (
            jnp.stack([grad_queries, grad_keys, grad_values])
            .reshape(3, length, heads * HD)
            .astype(jnp.bfloat16)
        )
        grad_qkv = jnp.einsum(
            "gd,jge->jde", normed_all, grad_mixed, preferred_element_type=jnp.float32
        )
        qkv_weight = w_qkv[layer]
        grad_normed = lax.psum_scatter(
            jnp.einsum(
                "jge,jde->gd", grad_mixed, qkv_weight, preferred_element_type=jnp.float32
            ).astype(jnp.bfloat16),
            "tensor",
            scatter_dimension=0,
            tiled=True,
        ).astype(jnp.float32)
        norm_pull = jax.vjp(layer_norm, rows_in, ln_gain[layer], ln_bias[layer])[1]
        grad_in_norm, grad_gain, grad_bias = norm_pull(grad_normed)
        gain_list[layer] = grad_gain
        bias_list[layer] = grad_bias
        grad_rows = grad_after + grad_in_norm
        qkv_list[layer] = grad_qkv
        out_list[layer] = grad_out
        up_list[layer] = grad_up
        down_list[layer] = grad_down
    grad_low = grad_rows.astype(jnp.bfloat16)
    grad_tokens = jnp.dot(grad_low, self_top.T, preferred_element_type=jnp.float32)
    grad_self = jnp.dot(joined.T, grad_low, preferred_element_type=jnp.float32)
    stacked_qkv = jnp.stack(qkv_list)
    stacked_out = jnp.stack(out_list)
    stacked_up = jnp.stack(up_list)
    stacked_down = jnp.stack(down_list)
    stacked_qkv, stacked_out, stacked_up, stacked_down = (
        lax.psum_scatter(stacked_qkv, "dp", scatter_dimension=2, tiled=True),
        lax.psum_scatter(stacked_out, "dp", scatter_dimension=2, tiled=True),
        lax.psum_scatter(stacked_up, "dp", scatter_dimension=1, tiled=True),
        lax.psum_scatter(stacked_down, "dp", scatter_dimension=2, tiled=True),
    )
    slot_grads = jnp.stack(slot_list)
    local_ada = jnp.einsum("sd,lse->lde", temb, slot_grads, precision=hp)
    local_ada_bias = jnp.sum(slot_grads, axis=1)
    shared = lax.psum(
        (
            local_ada,
            local_ada_bias,
            jnp.stack(gain_list),
            jnp.stack(bias_list),
            jnp.stack(down_bias_list),
            grad_self,
        ),
        ("dp", "tensor"),
    )
    stacked_ada, stacked_ada_bias, sum_gain, sum_bias, sum_down_bias, sum_self = shared
    return (
        activations,
        grad_tokens,
        sum_gain,
        sum_bias,
        stacked_qkv,
        stacked_out,
        stacked_ada,
        stacked_ada_bias,
        stacked_up,
        stacked_down,
        sum_down_bias,
        sum_self,
    )


def solution(mesh):
    return jax.shard_map(
        local,
        mesh=mesh,
        in_specs=(
            P(("dp", "tensor"), None),
            P(("dp", "tensor"), None),
            P("dp", None),
            P("dp", None),
            P(),
            P(),
            P(),
            P(None, None, None, "tensor"),
            P(None, "tensor", None),
            P(),
            P(),
            P(None, None, "tensor"),
            P(None, "tensor", None),
            P(),
        ),
        out_specs=(
            P(("dp", "tensor"), None),
            P(("dp", "tensor"), None),
            P(),
            P(),
            P(None, None, "dp", "tensor"),
            P(None, "tensor", "dp"),
            P(),
            P(),
            P(None, "dp", "tensor"),
            P(None, "tensor", "dp"),
            P(),
            P(),
        ),
        check_vma=False,
    )
```

profile of v0, /device:TPU:5, one launch (start us, length us, event | category | flops | bytes accessed | tf_op | source)
XLA Modules:
  0.0 1598.8 jit_solution(4170018935681315384)
XLA Ops:
  15.4 15.4 all-gather.13.cloned.1.call-done
  36.2 20.3 %while.74 = (s32[]{:T(128)}, bf16[2,512,3,64]{1,3,2,0:T(8,128)(2,1)S(1)}, pred[2,512,1024]{2,1,0:T(8,128)(4,1)S(1)}, bf16[2,512,3,64]{1,3,2,0:T(8,128)(2,1)}, bf...) while((s32[]{:T(128)}, bf16[2,512,3,64]{1,3,2,0:T(8,128)(2,1)S(1)}, ...), condition=%wide.region_8.9_spmd, body=%wide.region_5.8_spmd.sunk | while | flops 412091392 | bytes 15546465 | solution.py:92
  36.2 6.1 fusion.508
  42.4 3.9 fusion.509
  46.4 6.1 fusion.508
  52.5 3.9 fusion.509
  60.5 4.7 fusion.172
  66.7 20.2 %reduce-scatter.20.cloned.1.call-done = bf16[256,768]{1,0:T(8,128)(2,1)} async-done(((bf16[1024,768]{1,0:T(8,128)(2,1)}), bf16[256,768]{1,0:T(8,128)(2,1)}) %reduce-scatter.20.cloned.1.call-update) | async-done | bytes 393232 | tf_op jit(solution)/shard_map/reduce_scatter | solution.py:193
  91.3 20.0 %all-gather.15.cloned.1.call-done = bf16[1024,768]{1,0:T(8,128)(2,1)} async-done(((bf16[256,768]{1,0:T(8,128)(2,1)}), bf16[1024,768]{1,0:T(8,128)(2,1)}) %all-gather.15.cloned.1.call-update) | async-done | bytes 1572880 | tf_op jit(solution)/shard_map/all_gather | solution.py:204
  111.3 11.9 convolution_convert_fusion.8
  124.1 27.2 %reduce-scatter.22.cloned.1.call-done = bf16[256,768]{1,0:T(8,128)(2,1)} async-done(((bf16[1024,768]{1,0:T(8,128)(2,1)}), bf16[256,768]{1,0:T(8,128)(2,1)}) %reduce-scatter.22.cloned.1.call-update) | async-done | bytes 393232 | tf_op jit(solution)/shard_map/reduce_scatter | solution.py:226
  154.5 19.5 %all-gather.17.cloned.1.call-done = bf16[1024,768]{1,0:T(8,128)(2,1)} async-done(((bf16[256,768]{1,0:T(8,128)(2,1)}), bf16[1024,768]{1,0:T(8,128)(2,1)}) %all-gather.17.cloned.1.call-update) | async-done | bytes 1572880 | tf_op jit(solution)/shard_map/all_gather | solution.py:181
  179.6 20.2 %while.75 = (s32[]{:T(128)}, bf16[2,512,3,64]{1,3,2,0:T(8,128)(2,1)S(1)}, pred[2,512,1024]{2,1,0:T(8,128)(4,1)S(1)}, bf16[2,512,3,64]{1,3,2,0:T(8,128)(2,1)}, bf...) while((s32[]{:T(128)}, bf16[2,512,3,64]{1,3,2,0:T(8,128)(2,1)S(1)}, ...), condition=%wide.region_18.19_spmd, body=%wide.region_15.18_spmd.sunk | while | flops 412091392 | bytes 15546465 | solution.py:92
  179.6 6.1 fusion.513
  185.7 3.9 fusion.514
  189.8 6.1 fusion.513
  195.9 3.9 fusion.514
  203.2 4.7 fusion.175
  211.2 20.0 %reduce-scatter.24.cloned.1.call-done = bf16[256,768]{1,0:T(8,128)(2,1)} async-done(((bf16[1024,768]{1,0:T(8,128)(2,1)}), bf16[256,768]{1,0:T(8,128)(2,1)}) %reduce-scatter.24.cloned.1.call-update) | async-done | bytes 393232 | tf_op jit(solution)/shard_map/reduce_scatter | solution.py:193
  236.0 19.8 %all-gather.19.cloned.1.call-done = bf16[1024,768]{1,0:T(8,128)(2,1)} async-done(((bf16[256,768]{1,0:T(8,128)(2,1)}), bf16[1024,768]{1,0:T(8,128)(2,1)}) %all-gather.19.cloned.1.call-update) | async-done | bytes 1572880 | tf_op jit(solution)/shard_map/all_gather | solution.py:204
  255.8 11.9 convolution_convert_fusion.6
  267.8 28.1 %reduce-scatter.26.cloned.1.call-done = bf16[256,768]{1,0:T(8,128)(2,1)} async-done(((bf16[1024,768]{1,0:T(8,128)(2,1)}), bf16[256,768]{1,0:T(8,128)(2,1)}) %reduce-scatter.26.cloned.1.call-update) | async-done | bytes 393232 | tf_op jit(solution)/shard_map/reduce_scatter | solution.py:226
  301.5 19.6 %all-gather.21.cloned.1.call-done = bf16[1024,768]{1,0:T(8,128)(2,1)} async-done(((bf16[256,768]{1,0:T(8,128)(2,1)}), bf16[1024,768]{1,0:T(8,128)(2,1)}) %all-gather.21.cloned.1.call-update) | async-done | bytes 1572880 | tf_op jit(solution)/shard_map/all_gather | solution.py:181
  325.3 12.4 while.76
  342.4 28.0 %reduce-scatter.28.cloned.1.call-done = bf16[256,768]{1,0:T(8,128)(2,1)} async-done(((bf16[1024,768]{1,0:T(8,128)(2,1)}), bf16[256,768]{1,0:T(8,128)(2,1)}) %reduce-scatter.28.cloned.1.call-update) | async-done | bytes 393232 | tf_op jit(solution)/shard_map/reduce_scatter | solution.py:193
  373.1 20.0 %all-gather.23.cloned.1.call-done = bf16[1024,768]{1,0:T(8,128)(2,1)} async-done(((bf16[256,768]{1,0:T(8,128)(2,1)}), bf16[1024,768]{1,0:T(8,128)(2,1)}) %all-gather.23.cloned.1.call-update) | async-done | bytes 1572880 | tf_op jit(solution)/shard_map/all_gather | solution.py:204
  393.1 11.4 multiply_convert_fusion.3
  408.3 28.0 %reduce-scatter.30.cloned.1.call-done = bf16[256,768]{1,0:T(8,128)(2,1)} async-done(((bf16[1024,768]{1,0:T(8,128)(2,1)}), bf16[256,768]{1,0:T(8,128)(2,1)}) %reduce-scatter.30.cloned.1.call-update) | async-done | bytes 393232 | tf_op jit(solution)/shard_map/reduce_scatter | solution.py:226
  439.1 19.8 %all-gather.25.cloned.1.call-done = bf16[1024,768]{1,0:T(8,128)(2,1)} async-done(((bf16[256,768]{1,0:T(8,128)(2,1)}), bf16[1024,768]{1,0:T(8,128)(2,1)}) %all-gather.25.cloned.1.call-update) | async-done | bytes 1572880 | tf_op jit(solution)/shard_map/all_gather | solution.py:181
  464.4 14.9 while.77
  482.3 28.0 %reduce-scatter.32.cloned.1.call-done = bf16[256,768]{1,0:T(8,128)(2,1)} async-done(((bf16[1024,768]{1,0:T(8,128)(2,1)}), bf16[256,768]{1,0:T(8,128)(2,1)}) %reduce-scatter.32.cloned.1.call-update) | async-done | bytes 393232 | tf_op jit(solution)/shard_map/reduce_scatter | solution.py:193
  513.5 19.4 %all-gather.27.cloned.1.call-done = bf16[1024,768]{1,0:T(8,128)(2,1)} async-done(((bf16[256,768]{1,0:T(8,128)(2,1)}), bf16[1024,768]{1,0:T(8,128)(2,1)}) %all-gather.27.cloned.1.call-update) | async-done | bytes 1572880 | tf_op jit(solution)/shard_map/all_gather | solution.py:204
  532.9 11.6 multiply_convert_fusion.2
  544.5 9.6 all-gather.29.cloned.1.call-done
  554.1 5.8 add_convert_fusion.1
  563.7 4.3 convolution_convert_fusion.2
  568.1 23.7 %reduce-scatter.36.cloned.1.call-done = bf16[256,768]{1,0:T(8,128)(2,1)} async-done(((bf16[1024,768]{1,0:T(8,128)(2,1)}), bf16[256,768]{1,0:T(8,128)(2,1)}) %reduce-scatter.36.cloned.1.call-update) | async-done | bytes 393232 | tf_op jit(solution)/shard_map/reduce_scatter | solution.py:275
  593.2 29.1 %reduce-scatter.34.cloned.1.call-done = bf16[256,768]{1,0:T(8,128)(2,1)} async-done(((bf16[1024,768]{1,0:T(8,128)(2,1)}), bf16[256,768]{1,0:T(8,128)(2,1)}) %reduce-scatter.34.cloned.1.call-update) | async-done | bytes 393232 | tf_op jit(solution)/shard_map/reduce_scatter | solution.py:226
  627.4 19.6 %all-gather.31.cloned.1.call-done = bf16[1024,768]{1,0:T(8,128)(2,1)} async-done(((bf16[256,768]{1,0:T(8,128)(2,1)}), bf16[1024,768]{1,0:T(8,128)(2,1)}) %all-gather.31.cloned.1.call-update) | async-done | bytes 1572880 | tf_op jit(solution)/shard_map/all_gather | solution.py:287
  653.0 45.2 %while.78 = (s32[]{:T(128)}, f32[1024,3,64]{0,2,1:T(8,128)S(1)}, f32[1024,3,64]{0,2,1:T(8,128)}, f32[2,512,3,64]{1,0,3,2:T(2,128)}, bf16[2,512,3,64]{1,3,2,0:T(8...) while((s32[]{:T(128)}, f32[1024,3,64]{0,2,1:T(8,128)S(1)}, ...), condition=%wide.region_48.49_spmd.clone, body=%wide.region_46.48_spmd.clone.sunk | while | flops 1031305728 | bytes 56928416 | solution.py:140
  667.5 8.0 dynamic_update_slice.48
  677.5 4.1 fusion.536
  690.2 8.0 dynamic_update_slice.48
  707.6 27.9 %reduce-scatter.38.cloned.1.call-done = bf16[256,768]{1,0:T(8,128)(2,1)} async-done(((bf16[1024,768]{1,0:T(8,128)(2,1)}), bf16[256,768]{1,0:T(8,128)(2,1)}) %reduce-scatter.38.cloned.1.call-update) | async-done | bytes 393232 | tf_op jit(solution)/shard_map/reduce_scatter | solution.py:307
  743.2 20.0 %all-gather.33.cloned.1.call-done = bf16[1024,768]{1,0:T(8,128)(2,1)} async-done(((bf16[256,768]{1,0:T(8,128)(2,1)}), bf16[1024,768]{1,0:T(8,128)(2,1)}) %all-gather.33.cloned.1.call-update) | async-done | bytes 1572880 | tf_op jit(solution)/shard_map/all_gather | solution.py:268
  763.2 5.8 add_convert_fusion
  772.8 28.1 %reduce-scatter.40.cloned.1.call-done = bf16[256,768]{1,0:T(8,128)(2,1)} async-done(((bf16[1024,768]{1,0:T(8,128)(2,1)}), bf16[256,768]{1,0:T(8,128)(2,1)}) %reduce-scatter.40.cloned.1.call-update) | async-done | bytes 393232 | tf_op jit(solution)/shard_map/reduce_scatter | solution.py:275
  806.4 20.0 %all-gather.35.cloned.1.call-done = bf16[1024,768]{1,0:T(8,128)(2,1)} async-done(((bf16[256,768]{1,0:T(8,128)(2,1)}), bf16[1024,768]{1,0:T(8,128)(2,1)}) %all-gather.35.cloned.1.call-update) | async-done | bytes 1572880 | tf_op jit(solution)/shard_map/all_gather | solution.py:287
  832.4 41.5 %while.79 = (s32[]{:T(128)}, f32[1024,3,64]{0,2,1:T(8,128)S(1)}, f32[1024,3,64]{0,2,1:T(8,128)}, f32[2,512,3,64]{1,0,3,2:T(2,128)}, bf16[2,512,3,64]{1,3,2,0:T(8...) while((s32[]{:T(128)}, f32[1024,3,64]{0,2,1:T(8,128)S(1)}, ...), condition=%wide.region_57.58_spmd.clone, body=%wide.region_55.57_spmd.clone.sunk | while | flops 1031305728 | bytes 56928416 | solution.py:140
  844.9 8.1 dynamic_update_slice.49
  854.1 4.1 fusion.549
  865.8 8.1 dynamic_update_slice.49
  889.1 8.3 copy.95
  910.9 6.8 copy.99
  917.7 8.3 reshape.453
  929.1 10.0 convolution_bitcast_fusion
  955.9 128.2 %all-reduce.10.cloned.1.call-done = f32[2,768,768]{1,0,2:T(2,128)} async-done(((f32[2,768,768]{1,0,2:T(2,128)}), f32[2,768,768]{1,0,2:T(2,128)}) %all-reduce.10.cloned.1.call-update) | async-done | bytes 4718608
  1086.1 62.9 %reduce-scatter.48.cloned.1.call-done = f32[96,384]{1,0:T(8,128)} async-done(((f32[768,384]{1,0:T(8,128)}), f32[96,384]{1,0:T(8,128)}) %reduce-scatter.48.cloned.1.call-update) | async-done | bytes 147472
  1151.0 44.2 %all-reduce.5 = (f32[2,768]{1,0:T(2,128)}, f32[2,768]{1,0:T(2,128)}, f32[2,1536]{1,0:T(2,128)}, f32[2,768]{1,0:T(2,128)}) all-reduce(f32[2,768]{1,0:T(2,128)S(1)} %pad_maximum_fusion.26, f32[2,768]{1,0:T(2,128)S(1)} %pad_maximum_fusion.27, f32[2,1536]{1,0:T(2,128)S(1)} %fusion.275, ...), channel_id=1, replica_groups=mesh['dp'=8,'tensor'=4] {'dp','tensor'}, use_global_device_ids=true, to_apply=%region_63.64 | all-reduce | flops 7680 | bytes 61440 | tf_op jit(solution)/shard_map/psum | solution.py:340
  1197.9 35.2 %reduce-scatter.46.cloned.1.call-done = f32[96,1152]{1,0:T(8,128)} async-done(((f32[768,1152]{1,0:T(8,128)}), f32[96,1152]{1,0:T(8,128)}) %reduce-scatter.46.cloned.1.call-update) | async-done | bytes 442384
  1235.6 251.7 %all-reduce.12.cloned.1.call-done = (f32[2,768,1536]{1,2,0:T(8,128)}, f32[1536,768]{1,0:T(8,128)}) async-done(((f32[2,768,1536]{1,2,0:T(8,128)}, f32[1536,768]{1,0:T(8,128)}), (f32[2,768,1536]{1,2,0:T(8,128)}, f32[1536,768]{1,0:T(8,128)})) %all-reduce.12.cloned.1.call-update) | async-done | bytes 14155792 | tf_op jit(solution)/shard_map/psum | solution.py:340
  1487.3 9.6 copy.97
  1496.9 90.4 %reduce-scatter.44.cloned.1.call-done = f32[2,96,768]{2,1,0:T(8,128)} async-done(((f32[2,768,768]{2,1,0:T(8,128)}), f32[2,96,768]{2,1,0:T(8,128)}) %reduce-scatter.44.cloned.1.call-update) | async-done | bytes 589840 | tf_op jit(solution)/shard_map/reduce_scatter | solution.py:334
  1587.2 4.8 copy.238
  (571 shorter events, 257.5 us)
Async XLA Ops:
  7.2 23.6 %all-gather.13.cloned.1.call-start = ((), (), s32[]{:S(2)}) async-start(), calls=%async_computation.15 | async-start | bytes 1966080 | tf_op jit(solution)/shard_map/all_gather | solution.py:181
  9.5 143.4 %copy-start.65 = (f32[768]{0:T(1024)}, f32[768]{0:T(1024)S(1)}, u32[]{:S(2)}) copy-start(f32[768]{0:T(1024)S(1)} %get-tuple-element.672) | copy-start | bytes 9220
  9.6 143.4 %copy-start.77 = (f32[768]{0:T(1024)}, f32[768]{0:T(1024)S(1)}, u32[]{:S(2)}) copy-start(f32[768]{0:T(1024)S(1)} %get-tuple-element.480) | copy-start | bytes 9220
  10.5 76.3 %reduce-scatter.20.cloned.1.call-start = ((), (), s32[]{:S(2)}) async-start(), calls=%async_computation.16 | async-start | bytes 1966080 | tf_op jit(solution)/shard_map/reduce_scatter | solution.py:193
  12.2 450.4 %copy-start.22 = (f32[1024,32]{0,1:T(8,128)}, f32[1024,32]{0,1:T(8,128)S(1)}, u32[]{:S(2)}) copy-start(f32[1024,32]{0,1:T(8,128)S(1)} %get-tuple-element.662) | copy-start | bytes 393220
  58.8 52.6 %all-gather.15.cloned.1.call-start = ((), (), s32[]{:S(2)}) async-start(), calls=%async_computation.17 | async-start | bytes 1966080 | tf_op jit(solution)/shard_map/all_gather | solution.py:204
  59.9 143.2 %copy-start.68 = (f32[4,384]{1,0:T(4,128)}, f32[4,384]{1,0:T(4,128)S(1)}, u32[]{:S(2)}) copy-start(f32[4,384]{1,0:T(4,128)S(1)} %get-tuple-element.663) | copy-start | bytes 18436
  66.7 56.6 %copy-start.8 = (f32[256,1536]{1,0:T(8,128)}, f32[256,1536]{1,0:T(8,128)S(1)}, u32[]{:S(2)}) copy-start(f32[256,1536]{1,0:T(8,128)S(1)} %fusion.281) | copy-start | bytes 4718596
  91.3 60.1 %reduce-scatter.22.cloned.1.call-start = ((), (), s32[]{:S(2)}) async-start(), calls=%async_computation.18 | async-start | bytes 1966080 | tf_op jit(solution)/shard_map/reduce_scatter | solution.py:226
  123.3 50.7 %all-gather.17.cloned.1.call-start = ((), (), s32[]{:S(2)}) async-start(), calls=%async_computation.19 | async-start | bytes 1966080 | tf_op jit(solution)/shard_map/all_gather | solution.py:181
  124.1 52.6 %copy-start.81 = (f32[768]{0:T(1024)}, f32[768]{0:T(1024)S(1)}, u32[]{:S(2)}) copy-start(f32[768]{0:T(1024)S(1)} %get-tuple-element.477) | copy-start | bytes 9220
  124.1 171.7 %copy-start.83 = (f32[768]{0:T(1024)}, f32[768]{0:T(1024)S(1)}, u32[]{:S(2)}) copy-start(f32[768]{0:T(1024)S(1)} %get-tuple-element.476) | copy-start | bytes 9220
  153.9 77.3 %reduce-scatter.24.cloned.1.call-start = ((), (), s32[]{:S(2)}) async-start(), calls=%async_computation.20 | async-start | bytes 1966080 | tf_op jit(solution)/shard_map/reduce_scatter | solution.py:193
  203.1 52.8 %all-gather.19.cloned.1.call-start = ((), (), s32[]{:S(2)}) async-start(), calls=%async_computation.21 | async-start | bytes 1966080 | tf_op jit(solution)/shard_map/all_gather | solution.py:204
  235.8 60.1 %copy-start.24 = (bf16[256,768]{1,0:T(8,128)(2,1)S(1)}, bf16[256,768]{1,0:T(8,128)(2,1)}, u32[]{:S(2)}) copy-start(bf16[256,768]{1,0:T(8,128)(2,1)} %reduce-scatter.24.cloned.1.call-done) | copy-start | bytes 1179652
  235.8 60.1 %reduce-scatter.26.cloned.1.call-start = ((), (), s32[]{:S(2)}) async-start(), calls=%async_computation.22 | async-start | bytes 1966080 | tf_op jit(solution)/shard_map/reduce_scatter | solution.py:226
  267.7 53.4 %all-gather.21.cloned.1.call-start = ((), (), s32[]{:S(2)}) async-start(), calls=%async_computation.23 | async-start | bytes 1966080 | tf_op jit(solution)/shard_map/all_gather | solution.py:181
  299.8 70.6 %copy-start.4 = (f32[256,768]{1,0:T(8,128)}, f32[256,768]{1,0:T(8,128)S(1)}, u32[]{:S(2)}) copy-start(f32[256,768]{1,0:T(8,128)S(1)} %get-tuple-element.668) | copy-start | bytes 2359300
  301.1 69.3 %reduce-scatter.28.cloned.1.call-start = ((), (), s32[]{:S(2)}) async-start(), calls=%async_computation.24 | async-start | bytes 1966080 | tf_op jit(solution)/shard_map/reduce_scatter | solution.py:193
  337.7 34.0 %copy-start = (bf16[1024,3,64]{0,2,1:T(8,128)(2,1)}, bf16[1024,3,64]{0,2,1:T(8,128)(2,1)S(1)}, u32[]{:S(2)}) copy-start(bf16[1024,3,64]{0,2,1:T(8,128)(2,1)S(1)} %get-tuple-element.1190) | copy-start | bytes 1179652
  342.3 50.8 %all-gather.23.cloned.1.call-start = ((), (), s32[]{:S(2)}) async-start(), calls=%async_computation.25 | async-start | bytes 1966080 | tf_op jit(solution)/shard_map/all_gather | solution.py:204
  371.7 64.7 %copy-start.2 = (f32[256,768]{1,0:T(8,128)}, f32[256,768]{1,0:T(8,128)S(1)}, u32[]{:S(2)}) copy-start(f32[256,768]{1,0:T(8,128)S(1)} %get-tuple-element.595) | copy-start | bytes 2359300
  371.7 32.8 %copy-start.86 = (f32[256]{0:T(256)}, f32[256]{0:T(256)S(1)}, u32[]{:S(2)}) copy-start(f32[256]{0:T(256)S(1)} %broadcast_multiply_fusion.2) | copy-start | bytes 3076
  372.0 32.5 %copy-start.103 = (f32[256]{0:T(256)}, f32[256]{0:T(256)S(1)}, u32[]{:S(2)}) copy-start(f32[256]{0:T(256)S(1)} %multiply_reduce_fusion.6) | copy-start | bytes 3076
  372.0 32.5 %copy-start.109 = (f32[256]{0:T(256)}, f32[256]{0:T(256)S(1)}, u32[]{:S(2)}) copy-start(f32[256]{0:T(256)S(1)} %fusion.288) | copy-start | bytes 3076
  373.0 63.3 %reduce-scatter.30.cloned.1.call-start = ((), (), s32[]{:S(2)}) async-start(), calls=%async_computation.26 | async-start | bytes 1966080 | tf_op jit(solution)/shard_map/reduce_scatter | solution.py:226
  405.7 30.7 %copy-start.82 = (f32[768]{0:T(1024)S(1)}, f32[768]{0:T(1024)}, u32[]{:S(2)}) copy-start(f32[768]{0:T(1024)} %copy-done.81) | copy-start | bytes 9220
  408.3 29.6 %copy-start.66 = (f32[768]{0:T(1024)S(1)}, f32[768]{0:T(1024)}, u32[]{:S(2)}) copy-start(f32[768]{0:T(1024)} %copy-done.65) | copy-start | bytes 9220
  408.3 29.6 %copy-start.78 = (f32[768]{0:T(1024)S(1)}, f32[768]{0:T(1024)}, u32[]{:S(2)}) copy-start(f32[768]{0:T(1024)} %copy-done.77) | copy-start | bytes 9220
  408.3 50.6 %all-gather.25.cloned.1.call-start = ((), (), s32[]{:S(2)}) async-start(), calls=%async_computation.27 | async-start | bytes 1966080 | tf_op jit(solution)/shard_map/all_gather | solution.py:181
  438.8 71.5 %reduce-scatter.32.cloned.1.call-start = ((), (), s32[]{:S(2)}) async-start(), calls=%async_computation.28 | async-start | bytes 1966080 | tf_op jit(solution)/shard_map/reduce_scatter | solution.py:193
  482.3 50.7 %all-gather.27.cloned.1.call-start = ((), (), s32[]{:S(2)}) async-start(), calls=%async_computation.29 | async-start | bytes 1966080 | tf_op jit(solution)/shard_map/all_gather | solution.py:204
  512.9 41.3 %all-gather.29.cloned.1.call-start = ((), (), s32[]{:S(2)}) async-start(), calls=%async_computation.31 | async-start | bytes 1966080 | tf_op jit(solution)/shard_map/all_gather | solution.py:268
  513.4 78.3 %reduce-scatter.36.cloned.1.call-start = ((), (), s32[]{:S(2)}) async-start(), calls=%async_computation.32 | async-start | bytes 1966080 | tf_op jit(solution)/shard_map/reduce_scatter | solution.py:275
  563.7 58.7 %reduce-scatter.34.cloned.1.call-start = ((), (), s32[]{:S(2)}) async-start(), calls=%async_computation.30 | async-start | bytes 1966080 | tf_op jit(solution)/shard_map/reduce_scatter | solution.py:226
  568.0 54.3 %copy-start.84 = (f32[768]{0:T(1024)S(1)}, f32[768]{0:T(1024)}, u32[]{:S(2)}) copy-start(f32[768]{0:T(1024)} %copy-done.83) | copy-start | bytes 9220
  568.0 58.0 %copy-start.30 = (bf16[256,768]{1,0:T(8,128)(2,1)S(1)}, bf16[256,768]{1,0:T(8,128)(2,1)}, u32[]{:S(2)}) copy-start(bf16[256,768]{1,0:T(8,128)(2,1)} %param.27) | copy-start | bytes 1179652
  568.0 79.0 %all-gather.31.cloned.1.call-start = ((), (), s32[]{:S(2)}) async-start(), calls=%async_computation.33 | async-start | bytes 1966080 | tf_op jit(solution)/shard_map/all_gather | solution.py:287
  625.1 27.9 %copy-start.107 = (f32[256]{0:T(256)}, f32[256]{0:T(256)S(1)}, u32[]{:S(2)}) copy-start(f32[256]{0:T(256)S(1)} %negate_multiply_fusion.7) | copy-start | bytes 3076
  627.0 108.5 %reduce-scatter.38.cloned.1.call-start = ((), (), s32[]{:S(2)}) async-start(), calls=%async_computation.34 | async-start | bytes 1966080 | tf_op jit(solution)/shard_map/reduce_scatter | solution.py:307
  653.0 49.2 %copy-start.23 = (f32[1024,32]{0,1:T(8,128)S(1)}, f32[1024,32]{0,1:T(8,128)}, u32[]{:S(2)}) copy-start(f32[1024,32]{0,1:T(8,128)} %copy-done.22) | copy-start | bytes 393220
  704.7 30.7 %copy-start.67 = (f32[768]{0:T(1024)S(1)}, f32[768]{0:T(1024)}, u32[]{:S(2)}) copy-start(f32[768]{0:T(1024)} %copy-done.65) | copy-start | bytes 9220
  704.7 30.7 %copy-start.76 = (f32[256]{0:T(256)S(1)}, f32[256]{0:T(256)}, u32[]{:S(2)}) copy-start(f32[256]{0:T(256)} %copy-done.75) | copy-start | bytes 3076
  704.7 32.6 %copy-start.106 = (f32[256]{0:T(256)S(1)}, f32[256]{0:T(256)}, u32[]{:S(2)}) copy-start(f32[256]{0:T(256)} %copy-done.105) | copy-start | bytes 3076
  704.7 32.6 %copy-start.91 = (f32[256]{0:T(256)S(1)}, f32[256]{0:T(256)}, u32[]{:S(2)}) copy-start(f32[256]{0:T(256)} %copy-done.90) | copy-start | bytes 3076
  707.3 32.1 %copy-start.21 = (f32[256,768]{1,0:T(8,128)S(1)}, f32[256,768]{1,0:T(8,128)}, u32[]{:S(2)}) copy-start(f32[256,768]{1,0:T(8,128)} %copy-done.20) | copy-start | bytes 2359300
  707.3 32.1 %copy-start.31 = (bf16[256,768]{1,0:T(8,128)(2,1)S(1)}, bf16[256,768]{1,0:T(8,128)(2,1)}, u32[]{:S(2)}) copy-start(bf16[256,768]{1,0:T(8,128)(2,1)} %param.27) | copy-start | bytes 1179652
  707.3 32.1 %copy-start.108 = (f32[256]{0:T(256)S(1)}, f32[256]{0:T(256)}, u32[]{:S(2)}) copy-start(f32[256]{0:T(256)} %copy-done.107) | copy-start | bytes 3076
  707.4 55.8 %all-gather.33.cloned.1.call-start = ((), (), s32[]{:S(2)}) async-start(), calls=%async_computation.35 | async-start | bytes 1966080 | tf_op jit(solution)/shard_map/all_gather | solution.py:268
  743.2 57.7 %reduce-scatter.40.cloned.1.call-start = ((), (), s32[]{:S(2)}) async-start(), calls=%async_computation.36 | async-start | bytes 1966080 | tf_op jit(solution)/shard_map/reduce_scatter | solution.py:275
  770.1 30.7 %copy-start.3 = (f32[256,768]{1,0:T(8,128)S(1)}, f32[256,768]{1,0:T(8,128)}, u32[]{:S(2)}) copy-start(f32[256,768]{1,0:T(8,128)} %copy-done.2) | copy-start | bytes 2359300
  770.1 30.7 %copy-start.10 = (f32[256,1536]{1,0:T(8,128)S(1)}, f32[256,1536]{1,0:T(8,128)}, u32[]{:S(2)}) copy-start(f32[256,1536]{1,0:T(8,128)} %copy-done.8) | copy-start | bytes 4718596
  770.1 30.7 %copy-start.87 = (f32[256]{0:T(256)S(1)}, f32[256]{0:T(256)}, u32[]{:S(2)}) copy-start(f32[256]{0:T(256)} %copy-done.86) | copy-start | bytes 3076
  772.7 29.5 %copy-start.104 = (f32[256]{0:T(256)S(1)}, f32[256]{0:T(256)}, u32[]{:S(2)}) copy-start(f32[256]{0:T(256)} %copy-done.103) | copy-start | bytes 3076
  772.7 29.5 %copy-start.110 = (f32[256]{0:T(256)S(1)}, f32[256]{0:T(256)}, u32[]{:S(2)}) copy-start(f32[256]{0:T(256)} %copy-done.109) | copy-start | bytes 3076
  772.7 53.6 %all-gather.35.cloned.1.call-start = ((), (), s32[]{:S(2)}) async-start(), calls=%async_computation.37 | async-start | bytes 1966080 | tf_op jit(solution)/shard_map/all_gather | solution.py:287
  805.4 27.0 %copy-start.1 = (bf16[1024,3,64]{0,2,1:T(8,128)(2,1)S(1)}, bf16[1024,3,64]{0,2,1:T(8,128)(2,1)}, u32[]{:S(2)}) copy-start(bf16[1024,3,64]{0,2,1:T(8,128)(2,1)} %copy-done) | copy-start | bytes 1179652
  805.4 27.0 %copy-start.7 = (bf16[2,512,3,64]{1,3,2,0:T(8,128)(2,1)S(1)}, bf16[2,512,3,64]{1,3,2,0:T(8,128)(2,1)}, u32[]{:S(2)}) copy-start(bf16[2,512,3,64]{1,3,2,0:T(8,128)(2,1)} %copy-done.6) | copy-start | bytes 1179652
  806.3 132.7 %reduce-scatter.42.cloned.1.call-start = ((), (), s32[]{:S(2)}) async-start(), calls=%async_computation.38 | async-start | bytes 1966080 | tf_op jit(solution)/shard_map/reduce_scatter | solution.py:307
  881.9 202.3 %all-reduce.10.cloned.1.call-start = ((), (), s32[]{:S(2)}) async-start(), calls=%async_computation.42 | async-start | bytes 9437184
  897.4 251.6 %reduce-scatter.48.cloned.1.call-start = ((), (), s32[]{:S(2)}) async-start(), calls=%async_computation.41 | async-start | bytes 1327104
  904.8 328.2 %reduce-scatter.46.cloned.1.call-start = ((), (), s32[]{:S(2)}) async-start(), calls=%async_computation.40 | async-start | bytes 3981312
  926.0 561.3 %all-reduce.12.cloned.1.call-start = ((), (), s32[]{:S(2)}) async-start(), calls=%async_computation.43 | async-start | bytes 28311552 | tf_op jit(solution)/shard_map/psum | solution.py:340
  946.4 640.8 %reduce-scatter.44.cloned.1.call-start = ((), (), s32[]{:S(2)}) async-start(), calls=%async_computation.39 | async-start | bytes 5308416 | tf_op jit(solution)/shard_map/reduce_scatter | solution.py:334
  (95 other events, 559.9 us)
Sparse Core Ops, SparseCore 0:
  10.7 20.0 all-gather.12
  58.9 27.9 reduce-scatter.19
  91.4 19.9 all-gather.14
  123.4 27.9 reduce-scatter.21
  154.1 19.8 all-gather.16
  203.2 27.9 reduce-scatter.23
  235.9 19.9 all-gather.18
  267.9 27.9 reduce-scatter.25
  301.2 19.8 all-gather.20
  342.5 27.9 reduce-scatter.27
  373.1 19.9 all-gather.22
  408.4 27.9 reduce-scatter.29
  438.9 19.8 all-gather.24
  482.4 27.8 reduce-scatter.31
  513.0 19.8 all-gather.26
  534.4 19.6 all-gather.28
  563.8 27.9 reduce-scatter.35
  594.1 28.1 reduce-scatter.33
  627.1 19.8 all-gather.30
  707.5 27.9 reduce-scatter.37
  743.3 19.8 all-gather.32
  772.9 27.9 reduce-scatter.39
  806.4 19.9 all-gather.34
  882.0 27.9 reduce-scatter.41
  913.6 170.5 all-reduce.9
  1087.4 61.5 reduce-scatter.47
  1152.5 80.4 reduce-scatter.45
  1240.6 246.6 all-reduce.11
  1491.5 95.6 reduce-scatter.43
where the time goes:
time: 1610 us; the launch traced here: 1600 us
  waiting for transfers between devices  1080 us (67%)
  matrix products  257 us (16%)
  local copies, waits for them, and re-layouts  119 us (7%)
  other arithmetic  76.6 us (5%)
  blocking collectives  44.2 us (3%)
  between operations  17 us (1%)
    psum x1, waiting for transfers between devices, local(): lax.psum((local_ada, local_ada_bias, jnp.stack(gain_list), jnp.stack(bias...  252 us
    unnamed x32, waiting for transfers between devices  227 us
    reduce_scatter x4, waiting for transfers between devices, run_layers(): lax.psum_scatter(jnp.dot(gated, down_weight, preferred_element_type=jnp.f...  112 us
    reduce_scatter x4, waiting for transfers between devices, run_layers(): lax.psum_scatter(jnp.dot(attended, out_weight, preferred_element_type=jnp...  96.2 us
    reduce_scatter x1, waiting for transfers between devices, local(): lax.psum_scatter(stacked_up, 'dp', scatter_dimension=1, tiled=True)  90.4 us
    all_gather x4, waiting for transfers between devices, run_layers(): modulated_all = lax.all_gather(modulated, 'tensor', axis=0, tiled=True)  79.3 us
    all_gather x4, waiting for transfers between devices, run_layers(): normed_all = lax.all_gather(normed, 'tensor', axis=0, tiled=True)  74.3 us
    unnamed x273, local copies, waits for them, and re-layouts  54.4 us
  transfers between devices with their start and end apart: 29, of which 28 were waited for; matrix products, arithmetic and copies ran while one was open for 8% of the time, Pallas kernels for 0%

commit v1 on v0

v1 whole, which is shorter than its diff:
```python
import functools

import jax
import jax.numpy as jnp
from jax import lax
from jax.experimental import pallas as pl
from jax.experimental.pallas import tpu as pltpu
from jax.sharding import PartitionSpec as P

HD = 64
HALF = HD // 2
BF = jnp.bfloat16
F32 = jnp.float32
MESH = pl.DeviceIdType.MESH
EPS = 1e-05
LIMIT = 60 << 20


def norm(rows):
    centred = rows - jnp.mean(rows, axis=-1, keepdims=True)
    rstd = lax.rsqrt(jnp.mean(centred * centred, axis=-1, keepdims=True) + EPS)
    return (centred * rstd, rstd)


def norm_back(grad, hat, rstd):
    return rstd * (
        grad
        - jnp.mean(grad, axis=-1, keepdims=True)
        - hat * jnp.mean(grad * hat, axis=-1, keepdims=True)
    )


def dot(left, right, dims=((1,), (0,))):
    return lax.dot_general(left, right, (dims, ((), ())), preferred_element_type=F32)


NT = ((1,), (1,))
TN = ((0,), (0,))


def head_mask(head, rotary):
    lane = lax.broadcasted_iota(jnp.int32, (1, 256), 1)
    if rotary:
        return (lane % 128) // HALF == head
    return lane // HD == head


class Group:
    def __init__(self, sems, ids, gathered, pair_out, pair_in, own_out, own_in, far_out, far_in):
        self.sems = sems
        self.ids = ids
        self.gathered = gathered
        self.pair_out, self.pair_in = pair_out, pair_in
        self.own_out, self.own_in = own_out, own_in
        self.far_out, self.far_in = far_out, far_in
        self.half = gathered.shape[0] // 8

    def copy(self, src, dst, kind, part, far):
        send, recv = self.sems
        return pltpu.make_async_remote_copy(
            src_ref=src,
            dst_ref=dst,
            send_sem=send.at[kind, part],
            recv_sem=recv.at[kind, part],
            device_id=self.ids[1] if far else self.ids[0],
            device_id_type=MESH,
        )

    def rows(self, start):
        return pl.ds(pl.multiple_of(start, self.half), self.half)

    def pair(self, part):
        return 6 * self.half - 2 * self.half * part

    def far_copy(self, part):
        own = self.gathered.at[self.rows(part * self.half)]
        return self.copy(own, self.gathered.at[self.rows(self.pair(part))], 0, part, True)

    def sibling_copy(self, part):
        own = self.gathered.at[self.rows(part * self.half)]
        place = self.gathered.at[self.rows((2 + part) * self.half)]
        return self.copy(own, place, 1, part, False)

    def forward_copy(self, part):
        src = self.gathered.at[self.rows(self.pair(part))]
        dst = self.gathered.at[self.rows(self.pair(part) + self.half)]
        return self.copy(src, dst, 2, part, False)

    def send(self, part):
        self.far_copy(part).start()
        self.sibling_copy(part).start()

    def receive(self, step):
        @pl.when(step == 1)
        def _():
            self.sibling_copy(0).wait_recv()
            self.sibling_copy(1).wait_recv()

        @pl.when(step >= 2)
        def _():
            part = step - 2
            self.far_copy(part).wait_recv()
            self.forward_copy(part).start()
            self.forward_copy(part).wait_recv()

    def pair_copy(self, part):
        return self.copy(self.pair_out.at[part], self.pair_in.at[part], 3, part, False)

    def own_copy(self):
        return self.copy(self.own_out, self.own_in, 4, 0, False)

    def sum_copy(self, part):
        return self.copy(self.far_out.at[part], self.far_in.at[part], 5, part, True)

    def scatter(self, unit, total, own):
        @pl.when(unit == 0)
        def _():
            own[...] = total[...]

        @pl.when(unit == 1)
        def _():
            self.own_out[...] = total[...].astype(BF)
            self.own_copy().start()

        @pl.when(unit >= 2)
        def _():
            part = 3 - unit
            self.pair_out[part] = total[self.half :, :].astype(BF)
            self.pair_copy(part).start()
            self.pair_copy(part).wait_recv()
            self.far_out[part] = (
                total[: self.half, :] + self.pair_in[part].astype(F32)
            ).astype(BF)
            self.sum_copy(part).start()

    def collect(self, part, own):
        if part == 0:
            self.own_copy().wait_recv()
        self.sum_copy(part).wait_recv()
        rows = pl.ds(part * self.half, self.half)
        return own[rows, :] + self.own_in[rows, :].astype(F32) + self.far_in[part].astype(F32)

    def finish(self):
        for part in range(2):
            self.far_copy(part).wait_send()
            self.sibling_copy(part).wait_send()
            self.forward_copy(part).wait_send()
            self.pair_copy(part).wait_send()
            self.sum_copy(part).wait_send()
        self.own_copy().wait_send()


def neighbours():
    group = lax.axis_index("dp")
    place = lax.axis_index("tensor")
    core = lax.rem(place, 2)
    return ((group, place + 1 - 2 * core), (group, lax.rem(place + 2, 4)))


def meet(ids):
    barrier = pltpu.get_barrier_semaphore()
    for device in ids:
        pl.semaphore_signal(barrier, inc=1, device_id=device, device_id_type=MESH)
    pl.semaphore_wait(barrier, 2)


def group_scratch(rows, width):
    half = rows // 8
    return [
        pltpu.VMEM((rows, width), BF),
        pltpu.VMEM((2, half, width), BF),
        pltpu.VMEM((2, half, width), BF),
        pltpu.VMEM((2 * half, width), BF),
        pltpu.VMEM((2 * half, width), BF),
        pltpu.VMEM((2, half, width), BF),
        pltpu.VMEM((2, half, width), BF),
    ]


def gelu_parts(hidden):
    cdf = 0.5 * (1.0 + lax.erf(hidden * (0.5**0.5)))
    density = jnp.exp(hidden * hidden * -0.5) * 0.3989422804014327
    return (hidden * cdf, cdf + hidden * density)


def forward_kernel(layer, save, heads, refs):
    (x_ref, gain_ref, bias_ref, cond_ref, bdown_ref, cos_ref, sin_ref, neg_ref) = refs[:8]
    hbm_weights = refs[8:12]
    count = 10 if save else 0
    next_ref = refs[12]
    saves = refs[13 : 13 + count]
    scratch = refs[13 + count :]
    weights = scratch[:4]
    (wqkv, wout, wup, wdown) = weights
    first = scratch[4:11]
    second = scratch[11:18]
    (qb, kb, vb, lse, ob, x1, gb, gpb, total, own) = scratch[18:28]
    (send, recv, send2, recv2, wsem, osem) = scratch[28:]
    ids = neighbours()
    meet(ids)
    loads = [
        pltpu.make_async_copy(src.at[layer], dst, wsem.at[i])
        for i, (src, dst) in enumerate(zip(hbm_weights, weights))
    ]
    for load in loads:
        load.start()
    attn = Group((send, recv), ids, *first)
    feed = Group((send2, recv2), ids, *second)
    abuf, mbuf = first[0], second[0]
    half = attn.half
    unit_rows = 2 * half
    width = x_ref.shape[1]
    for part in range(2):
        rows = pl.ds(part * half, half)
        hat = norm(x_ref[rows, :])[0]
        abuf[rows, :] = (hat * gain_ref[...] + bias_ref[...]).astype(BF)
        attn.send(part)
    loads[0].wait()

    def project(step, carry):
        attn.receive(step)
        unit = jnp.where(step < 2, step, 5 - step)
        rows = pl.ds(pl.multiple_of(unit * unit_rows, unit_rows), unit_rows)
        mixed = dot(abuf[rows, :], wqkv[...])
        cosine = cos_ref[rows, :]
        sine = sin_ref[rows, :]
        for place, dst, scale in ((0, qb, HD**-0.5), (256, kb, 1.0)):
            first_half = mixed[:, place : place + 128]
            second_half = mixed[:, place + 128 : place + 256]
            dst[rows, :128] = ((first_half * cosine - second_half * sine) * scale).astype(BF)
            dst[rows, 128:] = ((second_half * cosine + first_half * sine) * scale).astype(BF)
        vb[rows, :] = mixed[:, 512:].astype(BF)
        return carry

    lax.fori_loop(0, 4, project, 0)
    loads[1].wait()
    lane = lax.broadcasted_iota(jnp.int32, (1, 128), 1)

    def attend(step, carry):
        unit = 3 - step
        rows = pl.ds(pl.multiple_of(unit * unit_rows, unit_rows), unit_rows)
        queries = qb[rows, :]
        attended = jnp.zeros((unit_rows, 256), F32)
        logs = jnp.zeros((unit_rows, 128), F32)
        for head in range(heads):
            masked = jnp.where(head_mask(head, True), queries, jnp.zeros_like(queries))
            scores = dot(masked, kb[...], NT)
            scores = scores.reshape(2, half, 8 * half) + neg_ref[unit]
            scores = scores.reshape(unit_rows, 8 * half)
            largest = jnp.max(scores, axis=-1, keepdims=True)
            shares = jnp.exp(scores - largest)
            sums = jnp.sum(shares, axis=-1, keepdims=True)
            output = dot(shares.astype(BF), vb[...]) * (1.0 / sums)
            attended = jnp.where(head_mask(head, False), output, attended)
            if save:
                logs = jnp.where(lane == head, largest + jnp.log(sums), logs)
        if save:
            lse[unit] = logs.T[:8, :]
        attended = attended.astype(BF)
        ob[rows, :] = attended
        total[...] = dot(attended, wout[...])
        attn.scatter(unit, total, own)
        return carry

    lax.fori_loop(0, 4, attend, 0)
    loads[2].wait()
    loads[3].wait()
    shift = cond_ref[:, :width]
    scale = cond_ref[:, width:]
    for part in range(2):
        rows = pl.ds(part * half, half)
        after = x_ref[rows, :] + attn.collect(part, own)
        x1[rows, :] = after
        mbuf[rows, :] = (norm(after)[0] * (1.0 + scale) + shift).astype(BF)
        feed.send(part)

    def expand(step, carry):
        feed.receive(step)
        unit = jnp.where(step < 2, step, 5 - step)
        rows = pl.ds(pl.multiple_of(unit * unit_rows, unit_rows), unit_rows)
        hidden = dot(mbuf[rows, :], wup[...])
        gated, slope = gelu_parts(hidden)
        gated = gated.astype(BF)
        if save:
            gb[rows, :] = gated
            gpb[rows, :] = slope.astype(BF)
        total[...] = dot(gated, wdown[...])
        feed.scatter(unit, total, own)
        return carry

    lax.fori_loop(0, 4, expand, 0)
    stores = []
    if save:
        made = (abuf, qb, kb, vb, lse, ob, x1, mbuf, gb, gpb)
        for i, (src, dst) in enumerate(zip(made, saves)):
            stores.append(pltpu.make_async_copy(src, dst, osem.at[i]))
            stores[-1].start()
    for part in range(2):
        rows = pl.ds(part * half, half)
        next_ref[rows, :] = x1[rows, :] + feed.collect(part, own) + bdown_ref[...]
    attn.finish()
    feed.finish()
    for store in stores:
        store.wait()


def any_spec():
    return pl.BlockSpec(memory_space=pl.ANY)


def vmem_spec():
    return pl.BlockSpec(memory_space=pltpu.VMEM)


def forward_layer(layer, save, heads, rows, small, tables, weights):
    gain, bias, cond, bdown = small
    cosine, sine, neg = tables
    block, width = rows.shape
    length = 4 * block
    units = weights[2].shape[2]
    saved_shapes = [
        ((length, width), BF),
        ((length, 256), BF),
        ((length, 256), BF),
        ((length, 256), BF),
        ((4, 8, block), F32),
        ((length, 256), BF),
        ((block, width), F32),
        ((length, width), BF),
        ((length, units), BF),
        ((length, units), BF),
    ]
    out_shape = [jax.ShapeDtypeStruct((block, width), F32)]
    out_specs = [vmem_spec()]
    if save:
        out_shape += [jax.ShapeDtypeStruct(*each) for each in saved_shapes]
        out_specs += [any_spec()] * len(saved_shapes)
    scratch = [pltpu.VMEM(each.shape[1:], BF) for each in weights]
    scratch += group_scratch(length, width) + group_scratch(length, width)
    scratch += [
        pltpu.VMEM((length, 256), BF),
        pltpu.VMEM((length, 256), BF),
        pltpu.VMEM((length, 256), BF),
        pltpu.VMEM((4, 8, block), F32),
        pltpu.VMEM((length, 256), BF),
        pltpu.VMEM((block, width), F32),
        pltpu.VMEM((length, units) if save else (16, 128), BF),
        pltpu.VMEM((length, units) if save else (16, 128), BF),
        pltpu.VMEM((block, width), F32),
        pltpu.VMEM((block, width), F32),
    ]
    scratch += [pltpu.SemaphoreType.DMA((6, 2))] * 4
    scratch += [pltpu.SemaphoreType.DMA((4,)), pltpu.SemaphoreType.DMA((10,))]

    def kernel(*refs):
        forward_kernel(layer, save, heads, refs)

    return pl.pallas_call(
        kernel,
        out_shape=out_shape,
        in_specs=[vmem_spec()] * 8 + [any_spec()] * 4,
        out_specs=out_specs,
        scratch_shapes=scratch,
        compiler_params=pltpu.CompilerParams(
            collective_id=1 + 2 * layer + int(save), has_side_effects=True, vmem_limit_bytes=LIMIT
        ),
        name="layer_forward",
    )(rows, gain, bias, cond, bdown, cosine, sine, neg, *weights)


def backward_kernel(layer, heads, refs):
    (dx_ref, x_ref, x1_ref, gain_ref, cond_ref, cos_ref, sin_ref, neg_ref, lse_ref) = refs[:9]
    hbm = refs[9:21]
    (out_ref, small_ref, grads_ref) = refs[21:24]
    scratch = refs[24:]
    local = scratch[:12]
    (wqkv, wout, wup, wdown, abuf, qb, kb, vb, ob, mbuf, gb, gpb) = local
    first = scratch[12:19]
    second = scratch[19:26]
    (dhb, qmask, domask, dsb, pb, dqkv, total, own, dx1, grads) = scratch[26:36]
    (send, recv, send2, recv2, lsem, osem) = scratch[36:]
    ids = neighbours()
    meet(ids)
    order = (3, 11, 2, 9, 10, 1, 5, 6, 7, 0, 4, 8)
    loads = [
        pltpu.make_async_copy(src.at[layer] if i < 4 else src, dst, lsem.at[i])
        for i, (src, dst) in enumerate(zip(hbm, local))
    ]
    for i in order:
        loads[i].start()
    feed = Group((send, recv), ids, *first)
    attn = Group((send2, recv2), ids, *second)
    ebuf, fbuf = first[0], second[0]
    half = feed.half
    unit_rows = 2 * half
    width = x_ref.shape[1]
    for part in range(2):
        rows = pl.ds(part * half, half)
        ebuf[rows, :] = dx_ref[rows, :].astype(BF)
        feed.send(part)
    small_ref[...] = jnp.zeros_like(small_ref)
    small_ref[4:5, :] = jnp.sum(dx_ref[...], axis=0, keepdims=True)
    for i in (3, 11, 2):
        loads[i].wait()

    def contract(step, carry):
        feed.receive(step)
        unit = jnp.where(step < 2, step, 5 - step)
        rows = pl.ds(pl.multiple_of(unit * unit_rows, unit_rows), unit_rows)
        grad = dot(ebuf[rows, :], wdown[...], NT)
        grad = (grad * gpb[rows, :].astype(F32)).astype(BF)
        dhb[rows, :] = grad
        total[...] = dot(grad, wup[...], NT)
        feed.scatter(unit, total, own)
        return carry

    lax.fori_loop(0, 4, contract, 0)
    tiles = width // 256

    def outer(left, right, place, columns):
        def tile(index, carry):
            start = pl.multiple_of(index * 256, 256)
            grads[pl.ds(start, 256), place : place + columns] = dot(
                left[:, pl.ds(start, 256)], right[...], TN
            ).astype(BF)
            return carry

        lax.fori_loop(0, tiles, tile, 0)

    units = gb.shape[1]
    shift_sum = jnp.zeros((1, width), F32)
    scale_sum = jnp.zeros((1, width), F32)
    for part in range(2):
        if part == 0:
            loads[9].wait()
            loads[10].wait()
            outer(mbuf, dhb, 1024, units)
        else:
            outer(ebuf, gb, 1024 + units, units)
        rows = pl.ds(part * half, half)
        grad = feed.collect(part, own)
        hat, rstd = norm(x1_ref[rows, :])
        shift_sum += jnp.sum(grad, axis=0, keepdims=True)
        scale_sum += jnp.sum(grad * hat, axis=0, keepdims=True)
        after = dx_ref[rows, :] + norm_back(grad * (1.0 + cond_ref[:, width:]), hat, rstd)
        dx1[rows, :] = after
        fbuf[rows, :] = after.astype(BF)
        attn.send(part)
    small_ref[0:1, :] = shift_sum
    small_ref[1:2, :] = scale_sum
    for i in (1, 5, 6, 7):
        loads[i].wait()

    def turn_back(grad, rows, scale):
        cosine = cos_ref[rows, :]
        sine = sin_ref[rows, :]
        first_half = grad[:, :128]
        second_half = grad[:, 128:]
        return (
            ((first_half * cosine + second_half * sine) * scale).astype(BF),
            ((second_half * cosine - first_half * sine) * scale).astype(BF),
        )

    def attend(step, carry):
        attn.receive(step)
        unit = jnp.where(step < 2, step, 5 - step)
        rows = pl.ds(pl.multiple_of(unit * unit_rows, unit_rows), unit_rows)
        grad_out = dot(fbuf[rows, :], wout[...], NT).astype(BF)
        queries = qb[rows, :]
        grad_queries = jnp.zeros((unit_rows, 256), F32)
        for head in range(heads):
            masked = jnp.where(head_mask(head, True), queries, jnp.zeros_like(queries))
            masked_out = jnp.where(head_mask(head, False), grad_out, jnp.zeros_like(grad_out))
            start = pl.multiple_of((unit * heads + head) * unit_rows, unit_rows)
            place = pl.ds(start, unit_rows)
            qmask[place, :] = masked
            domask[place, :] = masked_out
            scores = dot(kb[...], masked, NT).reshape(8, half, unit_rows)
            shares = jnp.exp(scores - (lse_ref[unit, head : head + 1, :] - neg_ref[unit]))
            shares = shares.reshape(8 * half, unit_rows)
            grad_shares = dot(vb[...], masked_out, NT)
            centre = jnp.sum(shares * grad_shares, axis=0, keepdims=True)
            grad_scores = (shares * (grad_shares - centre)).astype(BF)
            pb[:, place] = shares.astype(BF)
            dsb[:, place] = grad_scores
            keys = jnp.where(head_mask(head, True), kb[...], jnp.zeros(kb.shape, BF))
            grad_queries = grad_queries + dot(grad_scores, keys, TN)
        low, high = turn_back(grad_queries, rows, HD**-0.5)
        dqkv[rows, :128] = low
        dqkv[rows, 128:256] = high
        return carry

    lax.fori_loop(0, 4, attend, 0)
    loads[0].wait()

    def spread(step, carry):
        unit = 3 - step
        rows = pl.ds(pl.multiple_of(unit * unit_rows, unit_rows), unit_rows)
        low, high = turn_back(dot(dsb[rows, :], qmask[...]), rows, 1.0)
        dqkv[rows, 256:384] = low
        dqkv[rows, 384:512] = high
        dqkv[rows, 512:768] = dot(pb[rows, :], domask[...]).astype(BF)
        total[...] = dot(dqkv[rows, :], wqkv[...], NT)
        attn.scatter(unit, total, own)
        return carry

    lax.fori_loop(0, 4, spread, 0)
    gain_sum = jnp.zeros((1, width), F32)
    bias_sum = jnp.zeros((1, width), F32)
    for part in range(2):
        if part == 0:
            loads[4].wait()
            outer(abuf, dqkv, 0, 768)
        else:
            loads[8].wait()
            outer(fbuf, ob, 768, 256)
            store = pltpu.make_async_copy(grads, grads_ref, osem)
            store.start()
        rows = pl.ds(part * half, half)
        grad = attn.collect(part, own)
        hat, rstd = norm(x_ref[rows, :])
        gain_sum += jnp.sum(grad * hat, axis=0, keepdims=True)
        bias_sum += jnp.sum(grad, axis=0, keepdims=True)
        out_ref[rows, :] = dx1[rows, :] + norm_back(grad * gain_ref[...], hat, rstd)
    small_ref[2:3, :] = gain_sum
    small_ref[3:4, :] = bias_sum
    feed.finish()
    attn.finish()
    store.wait()


def backward_layer(layer, heads, grad_rows, rows, gain, cond, tables, weights, saved):
    cosine, sine, neg = tables
    (normed, queries, keys, values, logs, attended, after, modulated, gated, slope) = saved
    block, width = rows.shape
    length = 4 * block
    units = weights[2].shape[2]
    columns = 1024 + 2 * units
    held = [*weights, normed, queries, keys, values, attended, modulated, gated, slope]
    scratch = [pltpu.VMEM(each.shape[1:], BF) for each in weights]
    scratch += [pltpu.VMEM(each.shape, BF) for each in held[4:]]
    scratch += group_scratch(length, width) + group_scratch(length, width)
    scratch += [
        pltpu.VMEM((length, units), BF),
        pltpu.VMEM((heads * length, 256), BF),
        pltpu.VMEM((heads * length, 256), BF),
        pltpu.VMEM((length, heads * length), BF),
        pltpu.VMEM((length, heads * length), BF),
        pltpu.VMEM((length, 768), BF),
        pltpu.VMEM((block, width), F32),
        pltpu.VMEM((block, width), F32),
        pltpu.VMEM((block, width), F32),
        pltpu.VMEM((width, columns), BF),
    ]
    scratch += [pltpu.SemaphoreType.DMA((6, 2))] * 4
    scratch += [pltpu.SemaphoreType.DMA((12,)), pltpu.SemaphoreType.DMA]

    def kernel(*refs):
        backward_kernel(layer, heads, refs)

    return pl.pallas_call(
        kernel,
        out_shape=[
            jax.ShapeDtypeStruct((block, width), F32),
            jax.ShapeDtypeStruct((8, width), F32),
            jax.ShapeDtypeStruct((width, columns), BF),
        ],
        in_specs=[vmem_spec()] * 9 + [any_spec()] * 12,
        out_specs=[vmem_spec(), vmem_spec(), any_spec()],
        scratch_shapes=scratch,
        compiler_params=pltpu.CompilerParams(
            collective_id=9 + layer, has_side_effects=True, vmem_limit_bytes=LIMIT
        ),
        name="layer_backward",
    )(grad_rows, rows, after, gain, cond, cosine, sine, neg, logs, *held)


def rotary_columns(weights, heads):
    parts = weights.reshape(*weights.shape[:-1], heads, 2, HALF)
    parts = jnp.swapaxes(parts, -3, -2)
    parts = jnp.pad(parts, [(0, 0)] * (parts.ndim - 2) + [(0, 4 - heads), (0, 0)])
    return parts.reshape(*weights.shape[:-1], 256)


def plain_columns(grads, heads):
    parts = grads.reshape(*grads.shape[:-1], 2, 4, HALF)[..., :heads, :]
    return jnp.swapaxes(parts, -3, -2).reshape(*grads.shape[:-1], heads * HD)


def local(
    tokens,
    cotangent,
    lengths,
    timesteps,
    w_self,
    ln_gain,
    ln_bias,
    w_qkv,
    w_out,
    w_ada,
    b_ada,
    w_up,
    w_down,
    b_down,
):
    hp = lax.Precision.HIGHEST
    block, width = tokens.shape
    depth = w_qkv.shape[0]
    heads = w_qkv.shape[3] // HD
    units = w_up.shape[2]
    place = lax.axis_index("tensor")
    core = place % 2
    sibling = place + 1 - 2 * core
    far = (place + 2) % 4
    far_other = (sibling + 2) % 4
    half = block // 2
    owners = jnp.stack([place, place, sibling, sibling, far, far_other, far, far_other])
    halves = jnp.array([0, 1, 0, 1, 1, 1, 0, 0], jnp.int32)
    starts = owners * block + halves * half
    index = (starts[:, None] + jnp.arange(half, dtype=jnp.int32)).reshape(-1)
    packed = lengths[0, 0] < 4 * block
    position = jnp.where(packed, index % block, index)
    freqs = jnp.exp(-jnp.log(10000.0) * jnp.arange(HALF).astype(F32) / HALF)
    angle = position.astype(F32)[:, None] * freqs
    cosine = jnp.tile(jnp.cos(angle), (1, 4))
    sine = jnp.tile(jnp.sin(angle), (1, 4))
    chunk = jnp.array([0, 0, 1, 1, 2, 3, 2, 3], jnp.int32)
    apart = (chunk[:, None] != chunk[None, :]).astype(F32) * jnp.where(packed, -1e9, 0.0)
    neg_keys = jnp.repeat(apart, half, axis=1).reshape(4, 2, 1, 4 * block)
    neg_queries = jnp.repeat(apart, half, axis=1).reshape(8, 4, 1, block).swapaxes(0, 1)
    slot = jnp.where(packed, place, 0)
    freqs = jnp.exp(-jnp.log(10000.0) * jnp.arange(width // 2).astype(F32) / (width // 2))
    angle = lax.dynamic_slice_in_dim(timesteps, slot, 1, 1).astype(F32) * freqs
    temb = jnp.concatenate([jnp.cos(angle), jnp.sin(angle)], axis=-1)
    conds = [jnp.dot(temb, w_ada[l], precision=hp) + b_ada[l] for l in range(depth)]
    value_pad = [(0, 0), (0, 0), (0, 256 - heads * HD)]
    weights = (
        jnp.concatenate(
            [
                rotary_columns(w_qkv[:, 0], heads),
                rotary_columns(w_qkv[:, 1], heads),
                jnp.pad(w_qkv[:, 2], value_pad),
            ],
            axis=-1,
        ),
        jnp.pad(w_out, [(0, 0), (0, 256 - heads * HD), (0, 0)]),
        w_up,
        w_down,
    )

    def run(rows, save):
        kept = []
        for layer in range(depth):
            small = (
                ln_gain[layer][None],
                ln_bias[layer][None],
                conds[layer],
                b_down[layer][None],
            )
            made = forward_layer(
                layer, save, heads, rows, small, (cosine, sine, neg_keys), weights
            )
            kept.append((rows, made[1:]))
            rows = made[0]
        return (rows, kept)

    start = jnp.dot(tokens, w_self[:width], preferred_element_type=F32)
    estimate = run(start, False)[0].astype(BF)
    start = start + jnp.dot(estimate, w_self[width:], preferred_element_type=F32)
    rows, kept = run(start, True)
    activations = rows.astype(BF)
    grad_rows = cotangent.astype(F32)
    smalls = [None] * depth
    shards = [None] * depth
    for layer in reversed(range(depth)):
        rows_in, saved = kept[layer]
        grad_rows, smalls[layer], grads = backward_layer(
            layer,
            heads,
            grad_rows,
            rows_in,
            ln_gain[layer][None],
            conds[layer],
            (cosine, sine, neg_queries),
            weights,
            saved,
        )
        shards[layer] = lax.psum_scatter(grads, "dp", scatter_dimension=0, tiled=True).astype(F32)
    low = grad_rows.astype(BF)
    grad_tokens = dot(low, w_self[:width], NT)
    joined = jnp.concatenate([tokens, estimate], axis=1)
    grad_self = lax.psum(dot(joined, low, TN).astype(BF), ("dp", "tensor")).astype(F32)
    shard = jnp.stack(shards)
    grad_qkv = jnp.stack(
        [
            plain_columns(shard[..., :256], heads),
            plain_columns(shard[..., 256:512], heads),
            shard[..., 512 : 512 + heads * HD],
        ],
        axis=1,
    )
    grad_out = jnp.swapaxes(shard[..., 768 : 768 + heads * HD], 1, 2)
    grad_up = shard[..., 1024 : 1024 + units]
    grad_down = jnp.swapaxes(shard[..., 1024 + units :], 1, 2)
    vectors = jnp.concatenate([temb] + [each[:5].reshape(1, -1) for each in smalls], axis=1)
    vectors = lax.all_gather(vectors, ("dp", "tensor"), axis=0, tiled=True)
    times = vectors[:, :width]
    rest = vectors[:, width:].reshape(-1, depth, 5 * width)
    grad_ada = jnp.einsum("nd,nle->lde", times, rest[..., : 2 * width], precision=hp)
    sums = jnp.sum(rest, axis=0)
    return (
        activations,
        grad_tokens,
        sums[:, 2 * width : 3 * width],
        sums[:, 3 * width : 4 * width],
        grad_qkv,
        grad_out,
        grad_ada,
        sums[:, : 2 * width],
        grad_up,
        grad_down,
        sums[:, 4 * width :],
        grad_self,
    )


def solution(mesh):
    return jax.shard_map(
        local,
        mesh=mesh,
        in_specs=(
            P(("dp", "tensor"), None),
            P(("dp", "tensor"), None),
            P("dp", None),
            P("dp", None),
            P(),
            P(),
            P(),
            P(None, None, None, "tensor"),
            P(None, "tensor", None),
            P(),
            P(),
            P(None, None, "tensor"),
            P(None, "tensor", None),
            P(),
        ),
        out_specs=(
            P(("dp", "tensor"), None),
            P(("dp", "tensor"), None),
            P(),
            P(),
            P(None, None, "dp", "tensor"),
            P(None, "tensor", "dp"),
            P(),
            P(),
            P(None, "dp", "tensor"),
            P(None, "tensor", "dp"),
            P(),
            P(),
        ),
        check_vma=False,
    )
```

time: 1610 us -> 613 us (0.38)
  waiting for transfers between devices: 1080 us -> 229 us
  Pallas kernels: 0 us -> 288 us
  matrix products: 257 us -> 28.3 us
  local copies, waits for them, and re-layouts: 119 us -> 29.5 us
  other arithmetic: 76.6 us -> 16.3 us
  blocking collectives: 44.2 us -> 0 us
    reduce_scatter x13 -> x2, waiting for transfers between devices: 379 us -> 0.01 us  [local(): lax.psum_scatter(grads, 'dp', scatter_dimension=0, tiled=True).astype(F32)]
    pallas_call x0 -> x6, Pallas kernels: none -> 288 us  [the longest x4 185 us: forward_layer(): pl.pallas_call(kernel, out_shape=out_shape, in_specs=[vmem_spec()] * 8 +...]
    unnamed x32 -> x4, waiting for transfers between devices: 227 us -> 1.08 us
    dot_general x69 -> x7, matrix products: 222 us -> 28.3 us  [the longest x2 10.5 us: local(): jnp.dot(temb, w_ada[l], precision=hp) + b_ada[l]]
    all_gather x12 -> x1, waiting for transfers between devices: 223 us -> 55.8 us  [local(): vectors = lax.all_gather(vectors, ('dp', 'tensor'), axis=0, tiled=True)]
    psum x1, waiting for transfers between devices: 252 us -> 172 us  [local(): lax.psum(dot(joined, low, TN).astype(BF), ('dp', 'tensor')).astype(F32)]
    psum x1 -> x0, blocking collectives: 44.2 us -> none  [local(): lax.psum((local_ada, local_ada_bias, jnp.stack(gain_list), jnp.stack(bias...]
    unnamed x273 -> x47, local copies, waits for them, and re-layouts: 54.4 us -> 15 us
  transfers between devices with their start and end apart: 29 -> 4, of which waited for: 28 -> 2; matrix products, arithmetic and copies ran while one was open for 8% -> 5% of each run, Pallas kernels for 0% -> 0%
where the time goes in v1:
time: 613 us; the launch traced here: 608 us
  Pallas kernels  288 us (47%)
  waiting for transfers between devices  229 us (37%)
  local copies, waits for them, and re-layouts  29.5 us (5%)
  matrix products  28.3 us (5%)
  between operations  17 us (3%)
  other arithmetic  16.3 us (3%)
    pallas_call x4, Pallas kernels, forward_layer(): pl.pallas_call(kernel, out_shape=out_shape, in_specs=[vmem_spec()] * 8 +...  185 us
    psum x1, waiting for transfers between devices, local(): lax.psum(dot(joined, low, TN).astype(BF), ('dp', 'tensor')).astype(F32)  172 us
    pallas_call x2, Pallas kernels, backward_layer(): pl.pallas_call(kernel, out_shape=[jax.ShapeDtypeStruct((block, width), F3...  103 us
    all_gather x1, waiting for transfers between devices, local(): vectors = lax.all_gather(vectors, ('dp', 'tensor'), axis=0, tiled=True)  55.8 us
    unnamed x47, local copies, waits for them, and re-layouts  15 us
  transfers between devices with their start and end apart: 4, of which 2 were waited for; matrix products, arithmetic and copies ran while one was open for 5% of the time, Pallas kernels for 0%

profile of v1, /device:TPU:5, one launch (start us, length us, event | category | flops | bytes accessed | tf_op | source)
XLA Modules:
  0.0 608.4 jit_solution(10138984451521246706)
XLA Ops:
  8.0 0.0 all-reduce.6.cloned.1.call-start
  8.8 1.2 fusion.40
  10.0 0.7 fusion.31
  10.7 5.3 fusion.11.refs_3_.refs_4_
  16.0 5.3 fusion.8.refs_3_.refs_4_
  21.3 0.1 stack.43
  21.4 0.1 fusion.27
  21.5 0.6 fusion.39
  22.1 0.1 compare_select_fusion
  22.1 0.1 broadcast_in_dim.2
  22.2 0.6 copy.137
  22.9 0.5 multiply_sine_fusion
  23.5 1.0 copy.101.refs_6_
  24.5 1.0 copy.100.refs_5_
  25.5 1.0 convert_element_type.65.refs_0_
  26.5 2.4 fusion.34
  28.9 1.0 pad.18.refs_9_.refs_10_
  29.9 0.1 pad.15.clone
  30.0 0.3 copy.98
  30.3 1.0 pad.16.clone
  31.3 2.4 copy.99
  33.7 2.2 copy.126
  35.9 1.4 fusion.37
  37.4 1.4 fusion.17.refs_0_
  38.8 1.6 fusion.7.refs_8_.refs_9_
  40.4 45.4 %layer_forward.4.refs_0_ = f32[256,768]{1,0:T(8,128)} custom-call(f32[256,768]{1,0:T(8,128)} %fusion.17.refs_0_, f32[1,768]{1,0:T(1,128)} %get-tuple-element.135.refs_1_.refs_3_, f32[1,768]{1,0:T(1,128)} %get-tuple-element.140.refs_2_, f32[1,1536]{1,0:T(1,128)} %fusion.8.refs_3_.refs_4_, f32[1,768]{1,0:T(1,128)} %get-tuple-element.131.refs_4_, ...), custom_call_target="tpu_custom_call" | custom-call | tf_op jit(solution)/shard_map/layer_forward/pallas_call | solution.py:358
  85.8 46.5 %layer_forward.5 = f32[256,768]{1,0:T(8,128)} custom-call(f32[256,768]{1,0:T(8,128)} %layer_forward.4.refs_0_, f32[1,768]{1,0:T(1,128)} %get-tuple-element.134.refs_1_.refs_3_, f32[1,768]{1,0:T(1,128)} %get-tuple-element.141.refs_2_, f32[1,1536]{1,0:T(1,128)} %fusion.11.refs_3_.refs_4_, f32[1,768]{1,0:T(1,128)} %get-tuple-element.130.refs_4_, ...), custom_call_target="tpu_custom_call" | custom-call | tf_op jit(solution)/shard_map/layer_forward/pallas_call | solution.py:358
  132.4 1.2 convert_element_type.63
  133.6 1.4 convolution_add_fusion.refs_0_.refs_1_
  135.0 45.7 %layer_forward.6 = (f32[256,768]{1,0:T(8,128)}, bf16[1024,768]{1,0:T(8,128)(2,1)}, bf16[1024,256]{1,0:T(8,128)(2,1)}, bf16[1024,256]{1,0:T(8,128)(2,1)}, bf16[10...) custom-call(f32[256,768]{1,0:T(8,128)} %convolution_add_fusion.refs_, ...), custom_call_target="tpu_custom_call" | custom-call | tf_op jit(solution)/shard_map/layer_forward/pallas_call | solution.py:358
  180.7 47.0 %layer_forward.7 = (f32[256,768]{1,0:T(8,128)}, bf16[1024,768]{1,0:T(8,128)(2,1)}, bf16[1024,256]{1,0:T(8,128)(2,1)}, bf16[1024,256]{1,0:T(8,128)(2,1)}, bf16[10...) custom-call(f32[256,768]{1,0:T(8,128)} %get-tuple-element.40.refs_0_, ...), custom_call_target="tpu_custom_call" | custom-call | tf_op jit(solution)/shard_map/layer_forward/pallas_call | solution.py:358
  227.7 51.4 %layer_backward.2 = (f32[256,768]{1,0:T(8,128)}, f32[8,768]{1,0:T(8,128)}, bf16[768,2560]{1,0:T(8,128)(2,1)}) custom-call(f32[256,768]{1,0:T(8,128)} %convert_element_type.65.refs_0_, f32[256,768]{1,0:T(8,128)} %get-tuple-element.40.refs_0_.refs_1_, f32[256,768]{1,0:T(8,128)} %get-tuple-element.42.refs_2_, f32[1,768]{1,0:T(1,128)} %get-tuple-element.134.refs_1_.refs_3_, ...), custom_call_target="tpu_custom_call" | custom-call | tf_op jit(solution)/shard_map/layer_backward/pallas_call | solution.py:561
  279.1 51.6 %layer_backward.3 = (f32[256,768]{1,0:T(8,128)}, f32[8,768]{1,0:T(8,128)}, bf16[768,2560]{1,0:T(8,128)(2,1)}) custom-call(f32[256,768]{1,0:T(8,128)} %get-tuple-element.52.refs_0_, f32[256,768]{1,0:T(8,128)} %convolution_add_fusion.refs_0_.refs_1_, f32[256,768]{1,0:T(8,128)} %get-tuple-element.53.refs_2_, f32[1,768]{1,0:T(1,128)} %get-tuple-element.135.refs_1_.refs_3_, ...), custom_call_target="tpu_custom_call" | custom-call | tf_op jit(solution)/shard_map/layer_backward/pallas_call | solution.py:561
  330.7 3.4 convolution_convert_fusion
  334.1 0.0 all-reduce.6.cloned.1.call-update
  334.1 0.0 all-gather.3.cloned.1.call-start
  334.3 0.6 maximum_bitcast_fusion
  334.9 0.0 all-gather.3.cloned.1.call-update
  335.0 0.0 reduce-scatter.3.cloned.1.call-start
  335.0 0.5 reduce-scatter.3.cloned.1.call-update
  335.5 0.0 reduce-scatter.5.cloned.1.call-start
  335.6 0.5 reduce-scatter.5.cloned.1.call-update
  336.1 1.9 convert_element_type.64
  338.1 1.4 fusion.15
  339.4 172.4 %all-reduce.6.cloned.1.call-done = bf16[1536,768]{1,0:T(8,128)(2,1)} async-done(((bf16[1536,768]{1,0:T(8,128)(2,1)}), bf16[1536,768]{1,0:T(8,128)(2,1)}) %all-reduce.6.cloned.1.call-update) | async-done | bytes 2359312 | tf_op jit(solution)/shard_map/psum | solution.py:692
  511.8 4.2 convert_element_type.68
  516.0 55.8 %all-gather.3.cloned.1.call-done = f32[32,1,8448]{2,1,0:T(1,128)} async-done(((f32[1,1,8448]{2,1,0:T(1,128)}), f32[32,1,8448]{2,1,0:T(1,128)}) %all-gather.3.cloned.1.call-update) | async-done | bytes 1081360 | tf_op jit(solution)/shard_map/all_gather | solution.py:706
  571.8 1.3 copy.136
  573.1 0.1 fusion.35
  573.3 0.7 reshape.183
  574.0 0.6 slice.148
  574.6 10.3 %convolution_bitcast_fusion = f32[2,768,1536]{1,2,0:T(8,128)} fusion(f32[32,2,1536]{2,1,0:T(2,128)S(1)} %slice.146, f32[32,8448]{1,0:T(8,128)S(1)} %bitcast.98), kind=kOutput, calls=%fused_computation | convolution fusion | flops 905969664 | bytes 9928704 | tf_op jit(solution)/shard_map/nd,nle->lde/dot_general | solution.py:709
  584.9 9.6 %copy.122 = f32[2,768,1536]{2,1,0:T(8,128)} copy(f32[2,768,1536]{1,2,0:T(8,128)} %convolution_bitcast_fusion) | data formatting | bytes 18874368
  594.5 0.6 fusion.36
  595.1 1.0 convert_bitcast_fusion.1
  596.1 0.9 maximum_convert_fusion.2
  597.0 1.1 convert_bitcast_fusion
  598.1 0.8 copy.121
  598.9 0.1 copy.113
  599.1 0.1 copy.117
  599.2 0.1 copy.115
  599.4 0.1 copy.118
  599.5 0.1 pad_maximum_fusion
  599.6 0.9 copy.120
  (55 shorter events, 0.4 us)
Async XLA Ops:
  8.0 503.8 %all-reduce.6.cloned.1.call-start = ((), (), s32[]{:S(2)}) async-start(), calls=%async_computation.4 | async-start | bytes 4718592 | tf_op jit(solution)/shard_map/psum | solution.py:692
  10.7 5.3 copy-start.11
  16.0 5.4 copy-start.17
  16.0 5.5 copy-start.14
  16.0 6.1 copy-start.16
  21.3 4.2 copy-start.10
  22.2 1.2 copy-start.8
  26.5 2.5 copy-start.9
  30.3 5.6 copy-start.15
  30.3 7.1 %copy-start.1 = (bf16[1536,768]{1,0:T(8,128)(2,1)S(1)}, bf16[1536,768]{1,0:T(8,128)(2,1)}, u32[]{:S(2)}) copy-start(bf16[1536,768]{1,0:T(8,128)(2,1)} %param.20) | copy-start | bytes 7077892
  30.3 7.1 %copy-start.7 = (bf16[256,768]{1,0:T(8,128)(2,1)S(1)}, bf16[256,768]{1,0:T(8,128)(2,1)}, u32[]{:S(2)}) copy-start(bf16[256,768]{1,0:T(8,128)(2,1)} %param.16) | copy-start | bytes 1179652
  35.9 2.8 copy-start.4
  35.9 2.8 copy-start.5
  85.8 47.7 %copy-start = (f32[256,768]{1,0:T(8,128)S(1)}, f32[256,768]{1,0:T(8,128)}, u32[]{:S(2)}) copy-start(f32[256,768]{1,0:T(8,128)} %fusion.17.refs_0_) | copy-start | bytes 2359300
  330.7 3.5 copy-start.13
  330.7 3.5 copy-start.12
  334.1 237.7 %all-gather.3.cloned.1.call-start = ((), (), s32[]{:S(2)}) async-start(), calls=%async_computation.5 | async-start | bytes 1115136 | tf_op jit(solution)/shard_map/all_gather | solution.py:706
  335.0 260.1 %reduce-scatter.3.cloned.1.call-start = ((), (), s32[]{:S(2)}) async-start(), calls=%async_computation.2 | async-start | bytes 4423680 | tf_op jit(solution)/shard_map/reduce_scatter | solution.py:688
  335.5 259.6 %reduce-scatter.5.cloned.1.call-start = ((), (), s32[]{:S(2)}) async-start(), calls=%async_computation.3 | async-start | bytes 4423680 | tf_op jit(solution)/shard_map/reduce_scatter | solution.py:688
  335.6 2.5 copy-start.6
  595.1 1.9 copy-start.2
  595.1 1.9 copy-start.3
Sparse Core Ops, SparseCore 0:
  334.3 177.4 all-reduce.5
  515.8 56.0 all-gather.2
Sparse Core Ops, SparseCore 1:
  339.6 92.1 reduce-scatter.2
  435.3 88.1 reduce-scatter.4
